TPU v7x, 32 devices: a whole 2x2x4 slice. The times are simulated.
32 devices in a mesh: dp: 4 (over z), context: 4 (over x, core), tensor: 2 (over y).
Axes of the slice: x: 2, y: 2, z: 4, core: 2. Of those that a mesh axis runs over, the one named last changes fastest.
Arguments:
- hidden: bfloat16 [4, 1024, 1024], P('dp', 'context'), may hold values from -6 to 6
- cotangent: bfloat16 [4, 1024, 1024], P('dp', 'context'), may hold values from -6 to 6
- norm_gain: float32 [2, 1024], replicated, may hold values from 0.25 to 1.75
- inner_proj: bfloat16 [2, 1024, 2, 2048], P(None, 'dp', None, 'tensor'), may hold values from -0.1875 to 0.1875
- state_proj: bfloat16 [2, 1024, 256], P(None, 'dp'), may hold values from -0.1875 to 0.1875
- step_proj: bfloat16 [2, 1024, 32], P(None, 'dp', 'tensor'), may hold values from -0.1875 to 0.1875
- inner_conv: float32 [2, 4, 2048], P(None, None, 'tensor'), may hold values from -3 to 3
- inner_bias: float32 [2, 2048], P(None, 'tensor'), may hold values from -1.5 to 1.5
- state_conv: float32 [2, 4, 256], replicated, may hold values from -3 to 3
- state_bias: float32 [2, 256], replicated, may hold values from -1.5 to 1.5
- step_bias: float32 [2, 32], P(None, 'tensor'), may hold values from -7 to -3
- decay_log: float32 [2, 32], P(None, 'tensor'), may hold values from 0 to 1.5
- skip_gain: float32 [2, 32], P(None, 'tensor'), may hold values from 0.5 to 1.5
- gate_gain: float32 [2, 2048], P(None, 'tensor'), may hold values from 0.25 to 1.75
- out_proj: bfloat16 [2, 2048, 1024], P(None, 'tensor', 'dp'), may hold values from -0.125 to 0.125
Outputs:
- output: bfloat16 [4, 1024, 1024], P('dp', 'context')
- hidden_grad: bfloat16 [4, 1024, 1024], P('dp', 'context')
- prenorm_grad: float32 [2, 1024], replicated
- inner_grad: float32 [2, 1024, 2, 2048], P(None, 'dp', None, 'tensor')
- state_grad: float32 [2, 1024, 256], P(None, 'dp')
- step_grad: float32 [2, 1024, 32], P(None, 'dp', 'tensor')
- kernel_grad: float32 [2, 4, 2048], P(None, None, 'tensor')
- biases_grad: float32 [2, 2048], P(None, 'tensor')
- filters_grad: float32 [2, 4, 256], replicated
- offsets_grad: float32 [2, 256], replicated
- timebias_grad: float32 [2, 32], P(None, 'tensor')
- decay_grad: float32 [2, 32], P(None, 'tensor')
- skip_grad: float32 [2, 32], P(None, 'tensor')
- gate_grad: float32 [2, 2048], P(None, 'tensor')
- outer_grad: float32 [2, 2048, 1024], P(None, 'tensor', 'dp')
All inputs are finite; a program needn't handle non-finite values.
Results may differ from a plain program's by a relative error of at most 0.012.
The roundings to bfloat16 on the way count: a program that leaves them out, or rounds other values in their place, can miss the bound.
Values may be sent and summed in bfloat16 or wider, within the bound.
No kernel may reach another device: no remote copies, remote signals or barrier semaphores. Data moves between devices by JAX's collectives and lax.ppermute only.
A program may use at most 192 MiB of HBM per device.

v0:
```python
import jax
import jax.numpy as jnp
from jax import lax
from jax.sharding import PartitionSpec as P

eps_norm = 1e-05
highest = lax.Precision.HIGHEST


def from_behind(block, axis, distance):
    devices = range(lax.axis_size(axis))
    route = [(i - distance, i) for i in devices if i - distance in devices]
    return lax.ppermute(block, axis, route)


def carried_in(value, axis, join, neutral, backward):
    count, mine = (lax.axis_size(axis), lax.axis_index(axis))
    pieces = jax.tree.map(lambda part: lax.all_gather(part, axis), value)
    if backward:
        pieces = jax.tree.map(lambda part: part[::-1], pieces)
        mine = count - 1 - mine
    running = jax.tree.map(
        lambda part, zero: jnp.full_like(part, 0) + jnp.asarray(zero, part.dtype), value, neutral
    )

    def step(position, running):
        longer = join(running, jax.tree.map(lambda part: part[position], pieces))
        return jax.tree.map(lambda new, old: jnp.where(position < mine, new, old), longer, running)

    return lax.fori_loop(0, count - 1, step, running)


def silu_grad(inputs):
    sigmoid_value = jax.nn.sigmoid(inputs)
    return sigmoid_value * (1.0 + inputs * (1.0 - sigmoid_value))


def causal_conv(padded, kernel, offset, length_here):
    running = offset
    for shift_index in range(kernel.shape[0]):
        running = running + kernel[shift_index] * padded[:, shift_index : shift_index + length_here]
    return running


def conv_back(padded, kernel, gradient, length_here):
    support = kernel.shape[0]
    spread = jnp.zeros(padded.shape, jnp.float32)
    kernel_parts = []
    for shift_index in range(support):
        spread = spread + jnp.pad(
            kernel[shift_index] * gradient,
            ((0, 0), (shift_index, support - 1 - shift_index), (0, 0)),
        )
        kernel_parts.append(
            jnp.sum(padded[:, shift_index : shift_index + length_here] * gradient, axis=(0, 1))
        )
    return (spread, jnp.stack(kernel_parts), jnp.sum(gradient, axis=(0, 1)))


def link_states(earlier, latter):
    return (earlier[0] * latter[0], latter[0][:, :, None, None] * earlier[1] + latter[1])


def decay_table(cumulative):
    length_here = cumulative.shape[-1]
    row_index = lax.broadcasted_iota(jnp.int32, (length_here, length_here), 0)
    col_index = lax.broadcasted_iota(jnp.int32, (length_here, length_here), 1)
    causal = row_index >= col_index
    log_gaps = cumulative[..., :, None] - cumulative[..., None, :]
    return jnp.where(causal, jnp.exp(jnp.where(causal, log_gaps, 0.0)), 0.0)


def layer_forward(hidden_in, weights, params):
    inner_proj, state_proj, step_proj, out_proj = weights
    (
        norm_scale,
        inner_conv,
        inner_bias,
        state_conv,
        state_bias,
        step_bias,
        decay_log,
        skip_gain,
        gate_gain,
    ) = params
    batches, length_here, model_width = hidden_in.shape
    support = inner_conv.shape[0]
    heads_here = decay_log.shape[0]
    state_size = state_proj.shape[1] // 2
    norm_one = lax.rsqrt(jnp.mean(hidden_in * hidden_in, axis=-1, keepdims=True) + eps_norm)
    normed = (hidden_in * norm_one * norm_scale).astype(jnp.bfloat16)
    both_pre = jnp.einsum("std,dkc->stkc", normed, inner_proj, preferred_element_type=jnp.float32)
    gate_pre = both_pre[:, :, 0]
    inner_pre = both_pre[:, :, 1]
    state_pre = jnp.einsum("std,dc->stc", normed, state_proj, preferred_element_type=jnp.float32)
    step_pre = jnp.einsum("std,dh->sht", normed, step_proj, preferred_element_type=jnp.float32)
    edge_rows = from_behind(
        (inner_pre[:, length_here - support + 1 :], state_pre[:, length_here - support + 1 :]),
        "context",
        1,
    )
    inner_pad = jnp.concatenate([edge_rows[0], inner_pre], axis=1)
    state_pad = jnp.concatenate([edge_rows[1], state_pre], axis=1)
    inner_lin = causal_conv(inner_pad, inner_conv, inner_bias, length_here)
    state_lin = causal_conv(state_pad, state_conv, state_bias, length_here)
    heads_t = jnp.swapaxes(jax.nn.silu(inner_lin), 1, 2).reshape(
        batches, heads_here, -1, length_here
    )
    state_t = jnp.swapaxes(jax.nn.silu(state_lin), 1, 2)
    input_t = state_t[:, :state_size]
    output_t = state_t[:, state_size:]
    step_size = jax.nn.softplus(step_pre + step_bias[:, None])
    decay_rate = jnp.exp(decay_log)
    cumulative = jnp.cumsum(-step_size * decay_rate[:, None], axis=-1)
    decays = decay_table(cumulative)
    scores = jnp.einsum("snt,snu->stu", output_t, input_t, precision=highest)
    mixing = scores[:, None] * decays
    weighted = heads_t * step_size[:, :, None, :]
    intra_part = jnp.einsum("shtu,shpu->shpt", mixing, weighted, precision=highest)
    tail_decay = jnp.exp(cumulative[..., -1:] - cumulative)
    local_state = jnp.einsum(
        "shpu,snu->shpn", weighted * tail_decay[:, :, None, :], input_t, precision=highest
    )
    block_decay = jnp.exp(cumulative[..., -1])
    carried = carried_in(
        (block_decay, local_state),
        "context",
        link_states,
        (jnp.ones_like(block_decay), jnp.zeros_like(local_state)),
        False,
    )[1]
    rise_decay = jnp.exp(cumulative)
    inter_part = rise_decay[:, :, None, :] * jnp.einsum(
        "shpn,snt->shpt", carried, output_t, precision=highest
    )
    scan_heads = intra_part + inter_part + skip_gain[:, None, None] * heads_t
    scan_out = jnp.swapaxes(scan_heads.reshape(batches, -1, length_here), 1, 2)
    gate_act = jax.nn.silu(gate_pre)
    product = scan_out * gate_act
    inner_total = product.shape[-1] * lax.axis_size("tensor")
    squares = lax.psum(jnp.sum(product * product, axis=-1), "tensor")
    norm_two = lax.rsqrt(squares / inner_total + eps_norm)[..., None]
    normed_out = (product * norm_two * gate_gain).astype(jnp.bfloat16)
    partial_value = jnp.einsum(
        "stc,cd->std", normed_out, out_proj, preferred_element_type=jnp.float32
    )
    branch = lax.psum(partial_value, "tensor")
    stored = (
        hidden_in,
        norm_one,
        normed,
        gate_pre,
        inner_pad,
        state_pad,
        inner_lin,
        state_lin,
        step_pre,
        step_size,
        heads_t,
        weighted,
        input_t,
        output_t,
        cumulative,
        scores,
        tail_decay,
        block_decay,
        carried,
        rise_decay,
        inter_part,
        scan_out,
        gate_act,
        product,
        norm_two,
        normed_out,
    )
    return (hidden_in + branch, stored)


def layer_backward(gradient, weights, params, stored):
    inner_proj, state_proj, step_proj, out_proj = weights
    (
        norm_scale,
        inner_conv,
        inner_bias,
        state_conv,
        state_bias,
        step_bias,
        decay_log,
        skip_gain,
        gate_gain,
    ) = params
    (
        hidden_in,
        norm_one,
        normed,
        gate_pre,
        inner_pad,
        state_pad,
        inner_lin,
        state_lin,
        step_pre,
        step_size,
        heads_t,
        weighted,
        input_t,
        output_t,
        cumulative,
        scores,
        tail_decay,
        block_decay,
        carried,
        rise_decay,
        inter_part,
        scan_out,
        gate_act,
        product,
        norm_two,
        normed_out,
    ) = stored
    batches, length_here, model_width = hidden_in.shape
    support = inner_conv.shape[0]
    heads_here = decay_log.shape[0]
    inner_total = product.shape[-1] * lax.axis_size("tensor")
    grad_low = gradient.astype(jnp.bfloat16)
    outer_grad = jnp.einsum("stc,std->cd", normed_out, grad_low, preferred_element_type=jnp.float32)
    grad_normed_out = jnp.einsum(
        "std,cd->stc", grad_low, out_proj, preferred_element_type=jnp.float32
    )
    gate_grad = jnp.sum(grad_normed_out * product * norm_two, axis=(0, 1))
    scaled = grad_normed_out * gate_gain
    inner_dot = lax.psum(jnp.sum(scaled * product, axis=-1), "tensor")
    grad_product = norm_two * scaled - product * norm_two**3 * (inner_dot / inner_total)[..., None]
    grad_scan = jnp.swapaxes(grad_product * gate_act, 1, 2).reshape(
        batches, heads_here, -1, length_here
    )
    grad_gate = grad_product * scan_out * silu_grad(gate_pre)
    skip_grad = jnp.sum(grad_scan * heads_t, axis=(0, 2, 3))
    lifted = grad_scan * rise_decay[:, :, None, :]
    grad_output = jnp.einsum("shpn,shpt->snt", carried, lifted, precision=highest)
    grad_carried = jnp.einsum("shpt,snt->shpn", lifted, output_t, precision=highest)
    grad_cumul = jnp.sum(grad_scan * inter_part, axis=2)
    following = carried_in(
        (block_decay, grad_carried),
        "context",
        link_states,
        (jnp.ones_like(block_decay), jnp.zeros_like(grad_carried)),
        True,
    )[1]
    grad_block = jnp.sum(following * carried, axis=(2, 3))
    along_input = jnp.einsum("shpn,snu->shpu", following, input_t, precision=highest)
    grad_weighted = tail_decay[:, :, None, :] * along_input
    grad_input = jnp.einsum(
        "shpu,shpn->snu", weighted * tail_decay[:, :, None, :], following, precision=highest
    )
    grad_tail = jnp.sum(weighted * along_input, axis=2) * tail_decay
    last_extra = jnp.sum(grad_tail, axis=-1) + grad_block * block_decay
    decays = decay_table(cumulative)
    mixing = scores[:, None] * decays
    grad_mixing = jnp.einsum("shpt,shpu->shtu", grad_scan, weighted, precision=highest)
    grad_weighted = grad_weighted + jnp.einsum(
        "shtu,shpt->shpu", mixing, grad_scan, precision=highest
    )
    grad_scores = jnp.sum(grad_mixing * decays, axis=1)
    through = grad_mixing * mixing
    last_mark = (lax.broadcasted_iota(jnp.int32, (length_here,), 0) == length_here - 1).astype(
        jnp.float32
    )
    grad_cumul = (
        grad_cumul
        - grad_tail
        + jnp.sum(through, axis=3)
        - jnp.sum(through, axis=2)
        + last_extra[..., None] * last_mark
    )
    grad_output = grad_output + jnp.einsum("stu,snu->snt", grad_scores, input_t, precision=highest)
    grad_input = grad_input + jnp.einsum("stu,snt->snu", grad_scores, output_t, precision=highest)
    grad_rate = jnp.flip(jnp.cumsum(jnp.flip(grad_cumul, -1), axis=-1), -1)
    decay_rate = jnp.exp(decay_log)
    grad_steps = -grad_rate * decay_rate[:, None] + jnp.sum(grad_weighted * heads_t, axis=2)
    decay_grad = -jnp.sum(grad_rate * step_size, axis=(0, 2)) * decay_rate
    grad_heads = skip_gain[:, None, None] * grad_scan + grad_weighted * step_size[:, :, None, :]
    grad_step_pre = grad_steps * jax.nn.sigmoid(step_pre + step_bias[:, None])
    timebias_grad = jnp.sum(grad_step_pre, axis=(0, 2))
    grad_inner_lin = jnp.swapaxes(grad_heads.reshape(batches, -1, length_here), 1, 2) * silu_grad(
        inner_lin
    )
    grad_state_part = jnp.swapaxes(
        jnp.concatenate([grad_input, grad_output], axis=1), 1, 2
    ) * silu_grad(state_lin)
    grad_state_lin = lax.psum(grad_state_part, "tensor")
    inner_spread, kernel_grad, biases_grad = conv_back(
        inner_pad, inner_conv, grad_inner_lin, length_here
    )
    state_spread, filters_grad, offsets_grad = conv_back(
        state_pad, state_conv, grad_state_lin, length_here
    )
    arrived = from_behind(
        (inner_spread[:, : support - 1], state_spread[:, : support - 1]), "context", -1
    )
    tail_pad = ((0, 0), (length_here - support + 1, 0), (0, 0))
    grad_inner_pre = inner_spread[:, support - 1 :] + jnp.pad(arrived[0], tail_pad)
    grad_state_pre = (state_spread[:, support - 1 :] + jnp.pad(arrived[1], tail_pad)).astype(
        jnp.bfloat16
    )
    grad_both = jnp.stack([grad_gate, grad_inner_pre], axis=2).astype(jnp.bfloat16)
    grad_step_low = grad_step_pre.astype(jnp.bfloat16)
    inner_grad = jnp.einsum("std,stkc->dkc", normed, grad_both, preferred_element_type=jnp.float32)
    state_grad = jnp.einsum(
        "std,stc->dc", normed, grad_state_pre, preferred_element_type=jnp.float32
    )
    step_grad = jnp.einsum("std,sht->dh", normed, grad_step_low, preferred_element_type=jnp.float32)
    partial_in = jnp.einsum(
        "stkc,dkc->std", grad_both, inner_proj, preferred_element_type=jnp.float32
    ) + jnp.einsum("sht,dh->std", grad_step_low, step_proj, preferred_element_type=jnp.float32)
    grad_normed = lax.psum(partial_in, "tensor") + jnp.einsum(
        "stc,dc->std", grad_state_pre, state_proj, preferred_element_type=jnp.float32
    )
    prenorm_grad = jnp.sum(grad_normed * hidden_in * norm_one, axis=(0, 1))
    scaled_in = grad_normed * norm_scale
    grad_hidden = (
        gradient
        + norm_one * scaled_in
        - hidden_in * norm_one**3 * jnp.mean(scaled_in * hidden_in, axis=-1, keepdims=True)
    )
    large_part = (inner_grad, state_grad, step_grad, outer_grad)
    small_part = (
        prenorm_grad,
        kernel_grad,
        biases_grad,
        filters_grad,
        offsets_grad,
        timebias_grad,
        decay_grad,
        skip_grad,
        gate_grad,
    )
    return (grad_hidden, large_part, small_part)


def on_device(
    hidden,
    cotangent,
    norm_gain,
    inner_proj,
    state_proj,
    step_proj,
    inner_conv,
    inner_bias,
    state_conv,
    state_bias,
    step_bias,
    decay_log,
    skip_gain,
    gate_gain,
    out_proj,
):
    layers_here = inner_proj.shape[0]
    current = hidden.astype(jnp.float32)
    kept_weights = []
    kept_stored = []
    layer_params = []
    for layer_index in range(layers_here):
        weights = (
            lax.all_gather(inner_proj[layer_index], "dp", axis=0, tiled=True),
            lax.all_gather(state_proj[layer_index], "dp", axis=0, tiled=True),
            lax.all_gather(step_proj[layer_index], "dp", axis=0, tiled=True),
            lax.all_gather(out_proj[layer_index], "dp", axis=1, tiled=True),
        )
        params = (
            norm_gain[layer_index],
            inner_conv[layer_index],
            inner_bias[layer_index],
            state_conv[layer_index],
            state_bias[layer_index],
            step_bias[layer_index],
            decay_log[layer_index],
            skip_gain[layer_index],
            gate_gain[layer_index],
        )
        current, stored = layer_forward(current, weights, params)
        kept_weights.append(weights)
        kept_stored.append(stored)
        layer_params.append(params)
    output = current.astype(jnp.bfloat16)
    gradient = cotangent.astype(jnp.float32)
    large_grads = [None] * layers_here
    small_grads = [None] * layers_here
    for layer_index in reversed(range(layers_here)):
        weights = (
            lax.all_gather(inner_proj[layer_index], "dp", axis=0, tiled=True),
            lax.all_gather(state_proj[layer_index], "dp", axis=0, tiled=True),
            lax.all_gather(step_proj[layer_index], "dp", axis=0, tiled=True),
            lax.all_gather(out_proj[layer_index], "dp", axis=1, tiled=True),
        )
        gradient, large_part, small_part = layer_backward(
            gradient, weights, layer_params[layer_index], kept_stored[layer_index]
        )
        sliced = (
            lax.psum_scatter(large_part[0], "dp", scatter_dimension=0, tiled=True),
            lax.psum_scatter(large_part[1], "dp", scatter_dimension=0, tiled=True),
            lax.psum_scatter(large_part[2], "dp", scatter_dimension=0, tiled=True),
            lax.psum_scatter(large_part[3], "dp", scatter_dimension=1, tiled=True),
        )
        large_grads[layer_index] = lax.psum((sliced[0], sliced[1], sliced[2], sliced[3]), "context")
        small_grads[layer_index] = small_part
    stacked = [jnp.stack([member[position] for member in small_grads]) for position in range(9)]
    summed = lax.psum(
        (
            stacked[0],
            stacked[1],
            stacked[2],
            stacked[3],
            stacked[4],
            stacked[5],
            stacked[6],
            stacked[7],
            stacked[8],
        ),
        ("dp", "context"),
    )
    return (
        output,
        gradient.astype(jnp.bfloat16),
        summed[0],
        jnp.stack([member[0] for member in large_grads]),
        jnp.stack([member[1] for member in large_grads]),
        jnp.stack([member[2] for member in large_grads]),
        summed[1],
        summed[2],
        summed[3],
        summed[4],
        summed[5],
        summed[6],
        summed[7],
        summed[8],
        jnp.stack([member[3] for member in large_grads]),
    )


def solution(mesh):
    return jax.shard_map(
        on_device,
        mesh=mesh,
        in_specs=(
            P("dp", "context", None),
            P("dp", "context", None),
            P(),
            P(None, "dp", None, "tensor"),
            P(None, "dp", None),
            P(None, "dp", "tensor"),
            P(None, None, "tensor"),
            P(None, "tensor"),
            P(),
            P(),
            P(None, "tensor"),
            P(None, "tensor"),
            P(None, "tensor"),
            P(None, "tensor"),
            P(None, "tensor", "dp"),
        ),
        out_specs=(
            P("dp", "context", None),
            P("dp", "context", None),
            P(),
            P(None, "dp", None, "tensor"),
            P(None, "dp", None),
            P(None, "dp", "tensor"),
            P(None, None, "tensor"),
            P(None, "tensor"),
            P(),
            P(),
            P(None, "tensor"),
            P(None, "tensor"),
            P(None, "tensor"),
            P(None, "tensor"),
            P(None, "tensor", "dp"),
        ),
        check_vma=False,
    )
```

profile of v0, /device:TPU:0, one launch (start us, length us, event | category | flops | bytes accessed | tf_op | source)
XLA Modules:
  0.0 1502.0 jit_solution(12770364609541910137)
XLA Ops:
  13.0 21.1 %all-gather.2 = bf16[1,1024,256]{2,1,0:T(8,128)(2,1)S(1)} all-gather(bf16[1,256,256]{2,1,0:T(8,128)(2,1)S(1)} %get-tuple-element.879), channel_id=4, replica_groups=mesh['dp'=4,'context'=4,'tensor'=2] {'dp'}, dimensions={1}, use_global_device_ids=true | all-gather | bytes 655360 | tf_op jit(solution)/shard_map/all_gather | solution.py:365
  37.6 13.4 all-gather.1
  60.2 38.1 %all-gather.23.cloned.1.call-done = bf16[1,1024,2,1024]{3,1,2,0:T(8,128)(2,1)} async-done(((bf16[1,256,2,1024]{3,1,2,0:T(8,128)(2,1)}), bf16[1,1024,2,1024]{3,1,2,0:T(8,128)(2,1)}) %all-gather.23.cloned.1.call-update) | async-done | bytes 4194320 | tf_op jit(solution)/shard_map/all_gather | solution.py:364
  114.1 6.9 all-gather.3
  125.5 10.1 all-gather.25.cloned.1.call-done
  135.6 5.6 while.56
  143.0 6.2 fusion.79
  156.4 27.5 %all-gather.27.cloned.1.call-done = bf16[1,1024,1024]{2,1,0:T(8,128)(2,1)} async-done(((bf16[1,1024,256]{2,1,0:T(8,128)(2,1)}), bf16[1,1024,1024]{2,1,0:T(8,128)(2,1)}) %all-gather.27.cloned.1.call-update) | async-done | bytes 2097168 | tf_op jit(solution)/shard_map/all_gather | solution.py:367
  190.1 13.1 all-gather.7
  203.3 14.9 all-gather.8
  218.2 7.7 all-reduce.31.cloned.1.call-done
  235.1 73.1 %all-gather.29.cloned.1.call-done = bf16[1,1024,2,1024]{3,1,2,0:T(8,128)(2,1)} async-done(((bf16[1,256,2,1024]{3,1,2,0:T(8,128)(2,1)}), bf16[1,1024,2,1024]{3,1,2,0:T(8,128)(2,1)}) %all-gather.29.cloned.1.call-update) | async-done | bytes 4194320 | tf_op jit(solution)/shard_map/all_gather | solution.py:364
  350.3 8.9 all-gather.31.cloned.1.call-done
  364.0 7.7 fusion.88
  381.1 26.6 %all-gather.33.cloned.1.call-done = bf16[1,1024,1024]{2,1,0:T(8,128)(2,1)} async-done(((bf16[1,1024,256]{2,1,0:T(8,128)(2,1)}), bf16[1,1024,1024]{2,1,0:T(8,128)(2,1)}) %all-gather.33.cloned.1.call-update) | async-done | bytes 2097168 | tf_op jit(solution)/shard_map/all_gather | solution.py:367
  432.4 8.4 fusion.27
  452.1 7.5 while.58
  502.7 42.9 %all-reduce.39.cloned.1.call-done = (f32[1,256,1024]{2,1,0:T(8,128)}, f32[1,256,256]{2,1,0:T(8,128)}) async-done(((f32[1,256,1024]{2,1,0:T(8,128)}, f32[1,256,256]{2,1,0:T(8,128)}), (f32[1,256,1024]{2,1,0:T(8,128)}, f32[1,256,256]{2,1,0:T(8,128)})) %all-reduce.39.cloned.1.call-update) | async-done | bytes 1310736 | tf_op jit(solution)/shard_map/psum | solution.py:315
  580.3 8.6 fusion.25
  600.0 7.3 while.59
  639.5 66.0 %all-reduce.37.cloned.1.call-done = (f32[1,256,1024]{2,1,0:T(8,128)}, f32[1,256,1024]{2,1,0:T(8,128)}, f32[1,256,256]{2,1,0:T(8,128)}) async-done(((f32[1,256,1024]{2,1,0:T(8,128)}, f32[1,256,1024]{2,1,0:T(8,128)}, f32[1,256,256]{2,1,0:T(8,128)}), (f32[1,256,1024]{2,1,0:T(8,128)}, f32[1,256,1024]{2,1,0:T(8,128)}, f32[1,256,256]{2,1,0:T(8,128)})) %all-reduce.37.cloned.1.call-update) | async-done | bytes 2359312 | tf_op jit(solution)/shard_map/psum | solution.py:147
  729.0 6.0 reduce-scatter.15.cloned.1.call-done
  734.9 78.3 %reduce-scatter.23.cloned.1.call-done = f32[1024,256]{1,0:T(8,128)} async-done(((f32[1024,1024]{1,0:T(8,128)}), f32[1024,256]{1,0:T(8,128)}) %reduce-scatter.23.cloned.1.call-update) | async-done | bytes 1048592 | tf_op jit(solution)/shard_map/reduce_scatter | solution.py:402
  813.3 30.5 %reduce-scatter.13.cloned.1.call-done = f32[256,256]{1,0:T(8,128)} async-done(((f32[1024,256]{1,0:T(8,128)}), f32[256,256]{1,0:T(8,128)}) %reduce-scatter.13.cloned.1.call-update) | async-done | bytes 262160 | tf_op jit(solution)/shard_map/reduce_scatter | solution.py:400
  843.8 77.6 %reduce-scatter.21.cloned.1.call-done = f32[1024,256]{1,0:T(8,128)} async-done(((f32[1024,1024]{1,0:T(8,128)}), f32[1024,256]{1,0:T(8,128)}) %reduce-scatter.21.cloned.1.call-update) | async-done | bytes 1048592 | tf_op jit(solution)/shard_map/reduce_scatter | solution.py:402
  921.4 147.3 %reduce-scatter.11.cloned.1.call-done = f32[256,2,1024]{2,0,1:T(8,128)} async-done(((f32[1024,2,1024]{2,0,1:T(8,128)}), f32[256,2,1024]{2,0,1:T(8,128)}) %reduce-scatter.11.cloned.1.call-update) | async-done | bytes 2097168 | tf_op jit(solution)/shard_map/reduce_scatter | solution.py:399
  1068.7 147.6 %reduce-scatter.9.cloned.1.call-done = f32[256,2,1024]{2,0,1:T(8,128)} async-done(((f32[1024,2,1024]{2,0,1:T(8,128)}), f32[256,2,1024]{2,0,1:T(8,128)}) %reduce-scatter.9.cloned.1.call-update) | async-done | bytes 2097168 | tf_op jit(solution)/shard_map/reduce_scatter | solution.py:399
  1221.8 16.9 %reduce-scatter.19.cloned.1.call-done = f32[256,16]{0,1:T(8,128)} async-done(((f32[1024,16]{0,1:T(8,128)}), f32[256,16]{0,1:T(8,128)}) %reduce-scatter.19.cloned.1.call-update) | async-done | bytes 16400 | tf_op jit(solution)/shard_map/reduce_scatter | solution.py:401
  1238.8 20.0 %reduce-scatter.17.cloned.1.call-done = f32[256,16]{0,1:T(8,128)} async-done(((f32[1024,16]{0,1:T(8,128)}), f32[256,16]{0,1:T(8,128)}) %reduce-scatter.17.cloned.1.call-update) | async-done | bytes 16400 | tf_op jit(solution)/shard_map/reduce_scatter | solution.py:401
  1258.8 11.3 all-reduce.21
  1277.6 111.4 %all-reduce.35.cloned.1.call-done = (f32[1,256,2,1024]{3,1,2,0:T(8,128)}, f32[1,256,2,1024]{3,1,2,0:T(8,128)}, f32[1,256,256]{2,1,0:T(8,128)}, f32[1,256,256]{2,...) async-done(((f32[1,256,2,1024]{3,1,2,0:T(8,128)}, f32[1,256,2,1024]{3,1,2,0:T(8,128)}, f32[1,256,256]{2,1,0:T(8,128)}, f32[1,256,256]{2,1,0:T(8,128)}, ...) | async-done | bytes 6815760 | tf_op jit(solution)/shard_map/psum | solution.py:404
  1399.3 84.0 %all-reduce.33.cloned.1.call-done = (f32[2,1024]{1,0:T(2,128)}, f32[2,4,1024]{2,1,0:T(4,128)}, f32[2,1024]{1,0:T(2,128)}, f32[2,4,256]{2,1,0:T(4,128)}, f32[2,25...) async-done(((f32[2,1024]{1,0:T(2,128)}, f32[2,4,1024]{2,1,0:T(4,128)}, f32[2,1024]{1,0:T(2,128)}, ...) | async-done | bytes 67984 | tf_op jit(solution)/shard_map/psum | solution.py:407
  (746 shorter events, 355.4 us)
Async XLA Ops:
  7.2 91.1 %all-gather.23.cloned.1.call-start = ((), (), s32[]{:S(2)}) async-start(), calls=%async_computation.17 | async-start | bytes 5242880 | tf_op jit(solution)/shard_map/all_gather | solution.py:364
  12.1 123.5 %all-gather.25.cloned.1.call-start = ((), (), s32[]{:S(2)}) async-start(), calls=%async_computation.18 | async-start | bytes 2621440 | tf_op jit(solution)/shard_map/all_gather | solution.py:18
  35.7 68.7 %collective-permute-start.1 = (f32[1,3,256]{2,1,0:T(4,128)S(1)}, f32[1,3,256]{2,1,0:T(4,128)S(1)}, u32[]{:S(2)}, u32[]{:S(2)}) collective-permute-start(f32[1,3,256]{2,1,0:T(4,128)S(1)} %slice.400), channel_id=1, source_target_pairs={{0,2},{2,4},{4,6},{1,3},{3,5},{5,7},{8,10},{10,12},{12,14},{9,11},... | collective-permute-start | bytes 9224 | tf_op jit(solution)/shard_map/ppermute | solution.py:13
  102.0 3.3 collective-permute-start
  111.7 72.3 %all-gather.27.cloned.1.call-start = ((), (), s32[]{:S(2)}) async-start(), calls=%async_computation.19 | async-start | bytes 2621440 | tf_op jit(solution)/shard_map/all_gather | solution.py:367
  114.0 111.9 %all-reduce.31.cloned.1.call-start = ((), (), s32[]{:S(2)}) async-start(), calls=%async_computation.8 | async-start | bytes 2097152 | tf_op jit(solution)/shard_map/psum | solution.py:147
  187.5 120.8 %all-gather.29.cloned.1.call-start = ((), (), s32[]{:S(2)}) async-start(), calls=%async_computation.20 | async-start | bytes 5242880 | tf_op jit(solution)/shard_map/all_gather | solution.py:364
  190.1 169.1 %all-gather.31.cloned.1.call-start = ((), (), s32[]{:S(2)}) async-start(), calls=%async_computation.21 | async-start | bytes 2621440 | tf_op jit(solution)/shard_map/all_gather | solution.py:18
  232.1 94.9 %collective-permute-start.3 = (f32[1,3,256]{2,1,0:T(4,128)}, f32[1,3,256]{2,1,0:T(4,128)}, u32[]{:S(2)}, u32[]{:S(2)}) collective-permute-start(f32[1,3,256]{2,1,0:T(4,128)} %slice.416), channel_id=1, source_target_pairs={{0,2},{2,4},{4,6},{1,3},{3,5},{5,7},{8,10},{10,12},{12,14},{9,11},... | collective-permute-start | bytes 9224 | tf_op jit(solution)/shard_map/ppermute | solution.py:13
  313.1 15.7 %collective-permute-start.2 = (f32[1,3,1024]{2,1,0:T(4,128)S(1)}, f32[1,3,1024]{2,1,0:T(4,128)S(1)}, u32[]{:S(2)}, u32[]{:S(2)}) collective-permute-start(f32[1,3,1024]{2,1,0:T(4,128)S(1)} %slice.411), channel_id=1, source_target_pairs={{0,2},{2,4},{4,6},{1,3},{3,5},{5,7},{8,10},{10,12},{12,14},{9,11},... | collective-permute-start | bytes 36872 | tf_op jit(solution)/shard_map/ppermute | solution.py:13
  337.4 70.2 %all-gather.33.cloned.1.call-start = ((), (), s32[]{:S(2)}) async-start(), calls=%async_computation.22 | async-start | bytes 2621440 | tf_op jit(solution)/shard_map/all_gather | solution.py:367
  338.2 110.8 %all-gather.35.cloned.1.call-start = ((), (), s32[]{:S(2)}) async-start(), calls=%async_computation.23 | async-start | bytes 2621440 | tf_op jit(solution)/shard_map/all_gather | solution.py:18
  428.0 117.6 %all-reduce.39.cloned.1.call-start = ((), (), s32[]{:S(2)}) async-start(), calls=%async_computation.28 | async-start | bytes 2621440 | tf_op jit(solution)/shard_map/psum | solution.py:315
  491.0 3.8 collective-permute-start.4
  497.6 99.2 %all-gather.37.cloned.1.call-start = ((), (), s32[]{:S(2)}) async-start(), calls=%async_computation.24 | async-start | bytes 2621440 | tf_op jit(solution)/shard_map/all_gather | solution.py:18
  547.5 3.2 collective-permute-start.5
  572.9 132.6 %all-reduce.37.cloned.1.call-start = ((), (), s32[]{:S(2)}) async-start(), calls=%async_computation.27 | async-start | bytes 4718592 | tf_op jit(solution)/shard_map/psum | solution.py:147
  628.5 3.7 collective-permute-start.6
  635.0 99.9 %reduce-scatter.15.cloned.1.call-start = ((), (), s32[]{:S(2)}) async-start(), calls=%async_computation.12 | async-start | bytes 1310720 | tf_op jit(solution)/shard_map/reduce_scatter | solution.py:400
  636.5 176.7 %reduce-scatter.23.cloned.1.call-start = ((), (), s32[]{:S(2)}) async-start(), calls=%async_computation.16 | async-start | bytes 5242880 | tf_op jit(solution)/shard_map/reduce_scatter | solution.py:402
  639.5 204.3 %reduce-scatter.13.cloned.1.call-start = ((), (), s32[]{:S(2)}) async-start(), calls=%async_computation.11 | async-start | bytes 1310720 | tf_op jit(solution)/shard_map/reduce_scatter | solution.py:400
  707.3 3.0 collective-permute-start.7
  711.8 209.6 %reduce-scatter.21.cloned.1.call-start = ((), (), s32[]{:S(2)}) async-start(), calls=%async_computation.15 | async-start | bytes 5242880 | tf_op jit(solution)/shard_map/reduce_scatter | solution.py:402
  714.7 354.0 %reduce-scatter.11.cloned.1.call-start = ((), (), s32[]{:S(2)}) async-start(), calls=%async_computation.10 | async-start | bytes 10485760 | tf_op jit(solution)/shard_map/reduce_scatter | solution.py:399
  720.5 495.8 %reduce-scatter.9.cloned.1.call-start = ((), (), s32[]{:S(2)}) async-start(), calls=%async_computation.9 | async-start | bytes 10485760 | tf_op jit(solution)/shard_map/reduce_scatter | solution.py:399
  726.5 512.3 %reduce-scatter.19.cloned.1.call-start = ((), (), s32[]{:S(2)}) async-start(), calls=%async_computation.14 | async-start | bytes 81920 | tf_op jit(solution)/shard_map/reduce_scatter | solution.py:401
  727.9 542.8 %copy-start.183 = (f32[256]{0:T(256)S(1)}, f32[256]{0:T(256)}, u32[]{:S(2)}) copy-start(f32[256]{0:T(256)} %get-tuple-element.757) | copy-start | bytes 3076
  727.9 543.4 %copy-start.189 = (f32[256]{0:T(256)S(1)}, f32[256]{0:T(256)}, u32[]{:S(2)}) copy-start(f32[256]{0:T(256)} %get-tuple-element.756) | copy-start | bytes 3076
  727.9 544.0 %copy-start.3 = (f32[1,256,1024]{2,1,0:T(8,128)S(1)}, f32[1,256,1024]{2,1,0:T(8,128)}, u32[]{:S(2)}) copy-start(f32[1,256,1024]{2,1,0:T(8,128)} %copy-done.1) | copy-start | bytes 3145732
  727.9 530.9 %reduce-scatter.17.cloned.1.call-start = ((), (), s32[]{:S(2)}) async-start(), calls=%async_computation.13 | async-start | bytes 81920 | tf_op jit(solution)/shard_map/reduce_scatter | solution.py:401
  728.9 660.1 %all-reduce.35.cloned.1.call-start = ((), (), s32[]{:S(2)}) async-start(), calls=%async_computation.26 | async-start | bytes 13631488 | tf_op jit(solution)/shard_map/psum | solution.py:404
  1216.3 267.0 %all-reduce.33.cloned.1.call-start = ((), (), s32[]{:S(2)}) async-start(), calls=%async_computation.25 | async-start | bytes 141312 | tf_op jit(solution)/shard_map/psum | solution.py:407
  (202 other events, 9879.3 us)
Sparse Core Ops, SparseCore 0:
  12.2 86.0 all-gather.22
  111.8 23.6 all-gather.24
  137.7 46.2 all-gather.26
  187.6 38.2 all-reduce.30
  227.4 80.8 all-gather.28
  337.6 21.5 all-gather.30
  361.4 46.2 all-gather.32
  428.1 20.8 all-gather.34
  497.7 47.8 all-reduce.38
  573.1 22.7 all-gather.36
  635.2 70.3 all-reduce.36
  707.8 27.1 reduce-scatter.14
  737.8 75.4 reduce-scatter.22
  816.1 27.6 reduce-scatter.12
  845.9 75.4 reduce-scatter.20
  923.7 144.9 reduce-scatter.10
  1071.0 145.1 reduce-scatter.8
  1219.0 19.7 reduce-scatter.18
  1241.6 17.1 reduce-scatter.16
  1261.7 127.3 all-reduce.34
  1395.5 87.7 all-reduce.32
where the time goes:
time: 1510 us; the launch traced here: 1500 us
  waiting for transfers between devices  1020 us (68%)
  matrix products  131 us (9%)
  local copies, waits for them, and re-layouts  122 us (8%)
  blocking collectives  106 us (7%)
  other arithmetic  85.7 us (6%)
  between operations  17.4 us (1%)
  starting transfers between devices  15.1 us (1%)
    reduce_scatter x2, waiting for transfers between devices, on_device(): lax.psum_scatter(large_part[0], 'dp', scatter_dimension=0, tiled=True)  295 us
    reduce_scatter x2, waiting for transfers between devices, on_device(): lax.psum_scatter(large_part[3], 'dp', scatter_dimension=1, tiled=True)  156 us
    psum x1, waiting for transfers between devices, on_device(): lax.psum((sliced[0], sliced[1], sliced[2], sliced[3]), 'context')  111 us
    all_gather x2, waiting for transfers between devices, on_device(): lax.all_gather(inner_proj[layer_index], 'dp', axis=0, tiled=True)  111 us
    psum x1, waiting for transfers between devices, on_device(): lax.psum((stacked[0], stacked[1], stacked[2], stacked[3], stacked[4], sta...  84 us
    psum x2, waiting for transfers between devices, layer_forward(): branch = lax.psum(partial_value, 'tensor')  73.7 us
    all_gather x2, waiting for transfers between devices, on_device(): lax.all_gather(out_proj[layer_index], 'dp', axis=1, tiled=True)  54.1 us
    psum x1, waiting for transfers between devices, layer_backward(): lax.psum(partial_in, 'tensor')  42.9 us
  transfers between devices with their start and end apart: 29, of which 21 were waited for; matrix products, arithmetic and copies ran while one was open for 12% of the time, Pallas kernels for 0%

commit v1 on v0

v1 whole, which is shorter than its diff:
```python
import jax
import jax.numpy as jnp
from jax import lax
from jax.sharding import PartitionSpec as P

eps_norm = 1e-05
low = jnp.bfloat16
wide = jnp.float32


def swapped(value, axis, bit):
    return lax.ppermute(value, axis, [(i, i ^ bit) for i in range(lax.axis_size(axis))])


def shifted(value, axis, distance):
    count = lax.axis_size(axis)
    return lax.ppermute(
        value, axis, [(i, i + distance) for i in range(count) if 0 <= i + distance < count]
    )


def bits_of(axis):
    count = lax.axis_size(axis)
    assert count & (count - 1) == 0
    return [1 << k for k in range(count.bit_length() - 1)]


def spread(piece):
    pieces = {0: piece}
    for bit in reversed(bits_of("context")):
        for r in list(pieces):
            pieces[r | bit] = swapped(pieces[r], "context", bit)
    return [pieces[r] for r in range(len(pieces))]


def reduced(parts):
    parts = dict(enumerate(parts))
    for bit in bits_of("context"):
        for r in sorted(parts):
            if r & bit:
                parts[r ^ bit] = parts[r ^ bit] + swapped(
                    parts[r].astype(low), "context", bit
                ).astype(wide)
        parts = {r: part for r, part in parts.items() if not r & bit}
    return lax.psum_scatter(parts[0].astype(low), "dp", scatter_dimension=0, tiled=True)


def in_order(pieces):
    me = lax.axis_index("context")
    stacked = jnp.stack(pieces)
    return jnp.concatenate(
        [lax.dynamic_index_in_dim(stacked, q ^ me, keepdims=False) for q in range(len(pieces))]
    )


def to_local(value):
    me, count, shards = lax.axis_index("context"), lax.axis_size("context"), lax.axis_size("dp")
    lead = value.shape[:-1]
    cut = value.reshape(lead + (shards, count, -1))
    axis = len(lead) + 1
    return jnp.concatenate(
        [
            lax.dynamic_index_in_dim(cut, r ^ me, axis, keepdims=False).reshape(lead + (-1,))
            for r in range(count)
        ],
        axis=-1,
    )


def from_local(value):
    me, count, shards = lax.axis_index("context"), lax.axis_size("context"), lax.axis_size("dp")
    lead = value.shape[:-1]
    cut = value.reshape(lead + (count, shards, -1))
    axis = len(lead)
    return jnp.stack(
        [lax.dynamic_index_in_dim(cut, q ^ me, axis, keepdims=False) for q in range(count)],
        axis=axis + 1,
    ).reshape(value.shape)


def chunks(value):
    return jnp.split(value, lax.axis_size("context"), axis=-1)


def product_in(rows, pieces):
    total = 0.0
    for part, piece in zip(chunks(rows), pieces):
        total = total + jnp.dot(part, piece, preferred_element_type=wide)
    return total


def product_out(values, pieces):
    return jnp.concatenate(
        [
            lax.dot_general(values, piece, (((1,), (1,)), ((), ())), preferred_element_type=wide)
            for piece in pieces
        ],
        axis=-1,
    )


def product_grad(rows, values):
    return [
        lax.dot_general(part, values, (((0,), (0,)), ((), ())), preferred_element_type=wide)
        for part in chunks(rows)
    ]


def tensor_sum(value):
    mine = value.astype(low)
    total = mine.astype(wide)
    other = mine
    for bit in bits_of("tensor"):
        other = swapped(total.astype(low), "tensor", bit)
        total = total.astype(low).astype(wide) + other.astype(wide)
    return total


def chained(decay, value, direction):
    carried = jnp.zeros_like(value)
    count = lax.axis_size("context")
    for step in range(count - 1):
        source = step if direction == 1 else count - 1 - step
        sent = (decay * carried + value).astype(low)
        carried = carried + lax.ppermute(
            sent, "context", [(source, source + direction)]
        ).astype(wide)
    return carried


def silu_grad(inputs):
    sigmoid_value = jax.nn.sigmoid(inputs)
    return sigmoid_value * (1.0 + inputs * (1.0 - sigmoid_value))


def causal_conv(padded, kernel, offset):
    length_here = padded.shape[0] - kernel.shape[0] + 1
    running = offset
    for k in range(kernel.shape[0]):
        running = running + kernel[k] * padded[k : k + length_here]
    return running


def conv_back(padded, kernel, gradient):
    support, length_here = kernel.shape[0], gradient.shape[0]
    spread_rows = jnp.zeros(padded.shape, wide)
    kernel_parts = []
    for k in range(support):
        spread_rows = spread_rows + jnp.pad(kernel[k] * gradient, ((k, support - 1 - k), (0, 0)))
        kernel_parts.append(jnp.sum(padded[k : k + length_here] * gradient, axis=0))
    return (spread_rows, jnp.stack(kernel_parts), jnp.sum(gradient, axis=0))


def decay_table(cumulative):
    length_here = cumulative.shape[-1]
    row_index = lax.broadcasted_iota(jnp.int32, (length_here, length_here), 0)
    col_index = lax.broadcasted_iota(jnp.int32, (length_here, length_here), 1)
    causal = row_index >= col_index
    log_gaps = cumulative[..., :, None] - cumulative[..., None, :]
    return jnp.where(causal, jnp.exp(jnp.where(causal, log_gaps, 0.0)), 0.0)


def layer_forward(hidden_in, weights, params):
    scan_weights, gate_weights, out_weights = weights
    (norm_scale, taps, tap_bias, step_bias, decay_log, skip_gain, gate_gain) = params
    length_here = hidden_in.shape[0]
    support, inner = taps.shape[0], gate_gain.shape[0]
    heads_here = decay_log.shape[0]
    mixed = taps.shape[1]
    state_size = (mixed - inner) // 2
    norm_one = lax.rsqrt(jnp.mean(hidden_in * hidden_in, axis=-1, keepdims=True) + eps_norm)
    normed = (hidden_in * norm_one * norm_scale).astype(low)
    scan_pre = product_in(normed, scan_weights)
    conv_pre, step_pre = scan_pre[:, :mixed], scan_pre[:, mixed:].T
    edge_rows = shifted(conv_pre[length_here - support + 1 :], "context", 1)
    gate_pre = product_in(normed, gate_weights)
    padded = jnp.concatenate([edge_rows, conv_pre], axis=0)
    lin = causal_conv(padded, taps, tap_bias)
    acted = jax.nn.silu(lin)
    heads_t = acted[:, :inner].T.reshape(heads_here, -1, length_here)
    input_m = acted[:, inner : inner + state_size]
    output_m = acted[:, inner + state_size :]
    step_size = jax.nn.softplus(step_pre + step_bias[:, None])
    decay_rate = jnp.exp(decay_log)
    cumulative = jnp.cumsum(-step_size * decay_rate[:, None], axis=-1)
    tail_decay = jnp.exp(cumulative[..., -1:] - cumulative)
    weighted = heads_t * step_size[:, None, :]
    local_state = jnp.einsum("hpu,un->hpn", weighted * tail_decay[:, None, :], input_m)
    block_decay = jnp.exp(cumulative[:, -1])[:, None, None]
    carried = chained(block_decay, local_state, 1)
    decays = decay_table(cumulative)
    scores = jnp.dot(output_m, input_m.T)
    intra_part = jnp.einsum("htu,hpu->hpt", scores[None] * decays, weighted)
    rise_decay = jnp.exp(cumulative)
    inter_part = rise_decay[:, None, :] * jnp.einsum("hpn,tn->hpt", carried, output_m)
    scan_heads = intra_part + inter_part + skip_gain[:, None, None] * heads_t
    scan_out = scan_heads.reshape(-1, length_here).T
    gate_act = jax.nn.silu(gate_pre)
    product = scan_out * gate_act
    inner_total = inner * lax.axis_size("tensor")
    squares = jnp.sum(product * product, axis=-1)
    for bit in bits_of("tensor"):
        squares = squares + swapped(squares, "tensor", bit)
    norm_two = lax.rsqrt(squares / inner_total + eps_norm)[:, None]
    branch = tensor_sum(product_out((product * gate_gain).astype(low), out_weights))
    stored = (
        hidden_in, norm_one, normed, gate_pre, padded, lin, step_pre, step_size, heads_t, weighted,
        input_m, output_m, cumulative, scores, tail_decay, block_decay, carried, rise_decay,
        inter_part, scan_out, gate_act, product, norm_two, branch,
    )
    return (hidden_in + norm_two * branch, stored)


def layer_backward(gradient, weights, params, stored):
    scan_weights, gate_weights, out_weights = weights
    (norm_scale, taps, tap_bias, step_bias, decay_log, skip_gain, gate_gain) = params
    (
        hidden_in, norm_one, normed, gate_pre, padded, lin, step_pre, step_size, heads_t, weighted,
        input_m, output_m, cumulative, scores, tail_decay, block_decay, carried, rise_decay,
        inter_part, scan_out, gate_act, product, norm_two, branch,
    ) = stored
    length_here = hidden_in.shape[0]
    support, inner = taps.shape[0], gate_gain.shape[0]
    heads_here = decay_log.shape[0]
    inner_total = inner * lax.axis_size("tensor")
    grad_low = gradient.astype(low)
    normed_out = (product * norm_two * gate_gain).astype(low)
    outer_part = reduced(product_grad(grad_low, normed_out))
    grad_normed_out = product_in(grad_low, out_weights)
    gate_grad = jnp.sum(grad_normed_out * product * norm_two, axis=0)
    scaled = grad_normed_out * gate_gain
    inner_dot = jnp.sum(grad_low.astype(wide) * branch, axis=-1, keepdims=True)
    grad_product = norm_two * scaled - product * norm_two**3 * (inner_dot / inner_total)
    grad_scan = (grad_product * gate_act).T.reshape(heads_here, -1, length_here)
    grad_gate = (grad_product * scan_out * silu_grad(gate_pre)).astype(low)
    lifted = grad_scan * rise_decay[:, None, :]
    grad_carried = jnp.einsum("hpt,tn->hpn", lifted, output_m)
    following = chained(block_decay, grad_carried, -1)
    gate_part = reduced(product_grad(normed, grad_gate))
    skip_grad = jnp.sum(grad_scan * heads_t, axis=(1, 2))
    grad_output = jnp.einsum("hpn,hpt->tn", carried, lifted)
    grad_cumul = jnp.sum(grad_scan * inter_part, axis=1)
    decays = decay_table(cumulative)
    mixing = scores[None] * decays
    grad_mixing = jnp.einsum("hpt,hpu->htu", grad_scan, weighted)
    grad_scores = jnp.sum(grad_mixing * decays, axis=0)
    through = grad_mixing * mixing
    along_input = jnp.einsum("hpn,un->hpu", following, input_m)
    grad_weighted = tail_decay[:, None, :] * along_input + jnp.einsum(
        "htu,hpt->hpu", mixing, grad_scan
    )
    grad_block = jnp.sum(following * carried, axis=(1, 2))
    grad_input = jnp.einsum("hpu,hpn->un", weighted * tail_decay[:, None, :], following)
    grad_tail = jnp.sum(weighted * along_input, axis=1) * tail_decay
    last_extra = jnp.sum(grad_tail, axis=-1) + grad_block * block_decay[:, 0, 0]
    last_mark = (lax.broadcasted_iota(jnp.int32, (length_here,), 0) == length_here - 1).astype(wide)
    grad_cumul = (
        grad_cumul - grad_tail + jnp.sum(through, axis=2) - jnp.sum(through, axis=1)
        + last_extra[..., None] * last_mark
    )
    grad_output = grad_output + jnp.dot(grad_scores, input_m)
    grad_input = grad_input + jnp.dot(grad_scores.T, output_m)
    grad_rate = jnp.flip(jnp.cumsum(jnp.flip(grad_cumul, -1), axis=-1), -1)
    decay_rate = jnp.exp(decay_log)
    grad_steps = -grad_rate * decay_rate[:, None] + jnp.sum(grad_weighted * heads_t, axis=1)
    decay_grad = -jnp.sum(grad_rate * step_size, axis=1) * decay_rate
    grad_heads = skip_gain[:, None, None] * grad_scan + grad_weighted * step_size[:, None, :]
    grad_step_pre = grad_steps * jax.nn.sigmoid(step_pre + step_bias[:, None])
    timebias_grad = jnp.sum(grad_step_pre, axis=1)
    grad_lin = jnp.concatenate(
        [grad_heads.reshape(-1, length_here).T, grad_input, grad_output], axis=1
    ) * silu_grad(lin)
    spread_rows, taps_grad, tap_bias_grad = conv_back(padded, taps, grad_lin)
    arrived = shifted(spread_rows[: support - 1], "context", -1)
    grad_conv = spread_rows[support - 1 :] + jnp.pad(
        arrived, ((length_here - support + 1, 0), (0, 0))
    )
    grad_scan_pre = jnp.concatenate([grad_conv, grad_step_pre.T], axis=1).astype(low)
    scan_part = reduced(product_grad(normed, grad_scan_pre))
    grad_normed = tensor_sum(
        product_out(grad_scan_pre, scan_weights) + product_out(grad_gate, gate_weights)
    )
    prenorm_grad = jnp.sum(grad_normed * hidden_in * norm_one, axis=0)
    scaled_in = grad_normed * norm_scale
    grad_hidden = (
        gradient
        + norm_one * scaled_in
        - hidden_in * norm_one**3 * jnp.mean(scaled_in * hidden_in, axis=-1, keepdims=True)
    )
    state_part = scan_part[:, inner : taps.shape[1]].astype(wide)
    for bit in bits_of("tensor"):
        state_part = state_part + swapped(state_part.astype(low), "tensor", bit).astype(wide)
    large_part = (outer_part, gate_part, scan_part, state_part.astype(low))
    small_part = (
        from_local(prenorm_grad),
        taps_grad[:, :inner],
        tap_bias_grad[:inner],
        taps_grad[:, inner:],
        tap_bias_grad[inner:],
        timebias_grad,
        decay_grad,
        skip_grad,
        gate_grad,
    )
    return (grad_hidden, large_part, small_part)


def on_device(
    hidden,
    cotangent,
    norm_gain,
    inner_proj,
    state_proj,
    step_proj,
    inner_conv,
    inner_bias,
    state_conv,
    state_bias,
    step_bias,
    decay_log,
    skip_gain,
    gate_gain,
    out_proj,
):
    layers_here = inner_proj.shape[0]
    me, count = lax.axis_index("context"), lax.axis_size("context")
    rows = inner_proj.shape[1] // count

    def quarter(value, axis):
        return lax.dynamic_slice_in_dim(value, me * rows, rows, axis)

    inner_q, state_q, step_q = (quarter(v, 1) for v in (inner_proj, state_proj, step_proj))
    out_q = quarter(out_proj, 2)
    layer_weights = []
    for layer in range(layers_here):
        scan_q = jnp.concatenate([inner_q[layer, :, 1], state_q[layer], step_q[layer]], axis=1)
        layer_weights.append(
            [
                spread(lax.all_gather(piece, "dp", axis=0, tiled=True))
                for piece in (scan_q, inner_q[layer, :, 0], out_q[layer].T)
            ]
        )
    taps = jnp.concatenate([inner_conv, state_conv], axis=-1)
    tap_bias = jnp.concatenate([inner_bias, state_bias], axis=-1)
    gains = to_local(norm_gain)
    current = to_local(hidden[0]).astype(wide)
    kept_stored = []
    layer_params = []
    for layer in range(layers_here):
        layer_params.append(
            tuple(
                v[layer] for v in (gains, taps, tap_bias, step_bias, decay_log, skip_gain, gate_gain)
            )
        )
        current, stored = layer_forward(current, layer_weights[layer], layer_params[layer])
        kept_stored.append(stored)
    output = from_local(current.astype(low))
    gradient = to_local(cotangent[0]).astype(wide)
    large_grads = [None] * layers_here
    small_grads = [None] * layers_here
    for layer in reversed(range(layers_here)):
        gradient, large_part, small_grads[layer] = layer_backward(
            gradient, layer_weights[layer], layer_params[layer], kept_stored[layer]
        )
        large_grads[layer] = [in_order(spread(part)).astype(wide) for part in large_part]
    stacked = [jnp.stack([member[i] for member in small_grads]) for i in range(9)]
    everywhere = ("dp", "context", "tensor")
    filters_grad, offsets_grad = lax.psum((stacked[3], stacked[4]), everywhere)
    summed = lax.psum(
        tuple(v for i, v in enumerate(stacked) if i not in (3, 4)), ("dp", "context")
    )
    inner = gate_gain.shape[1]
    mixed = taps.shape[-1]
    return (
        output[None],
        from_local(gradient.astype(low))[None],
        summed[0],
        jnp.stack([jnp.stack([m[1], m[2][:, :inner]], axis=1) for m in large_grads]),
        jnp.stack([m[3] for m in large_grads]),
        jnp.stack([m[2][:, mixed:] for m in large_grads]),
        summed[1],
        summed[2],
        filters_grad,
        offsets_grad,
        summed[3],
        summed[4],
        summed[5],
        summed[6],
        jnp.stack([m[0].T for m in large_grads]),
    )


def solution(mesh):
    return jax.shard_map(
        on_device,
        mesh=mesh,
        in_specs=(
            P("dp", "context", None),
            P("dp", "context", None),
            P(),
            P(None, "dp", None, "tensor"),
            P(None, "dp", None),
            P(None, "dp", "tensor"),
            P(None, None, "tensor"),
            P(None, "tensor"),
            P(),
            P(),
            P(None, "tensor"),
            P(None, "tensor"),
            P(None, "tensor"),
            P(None, "tensor"),
            P(None, "tensor", "dp"),
        ),
        out_specs=(
            P("dp", "context", None),
            P("dp", "context", None),
            P(),
            P(None, "dp", None, "tensor"),
            P(None, "dp", None),
            P(None, "dp", "tensor"),
            P(None, None, "tensor"),
            P(None, "tensor"),
            P(),
            P(),
            P(None, "tensor"),
            P(None, "tensor"),
            P(None, "tensor"),
            P(None, "tensor"),
            P(None, "tensor", "dp"),
        ),
        check_vma=False,
    )
```

time: 1510 us -> 704 us (0.47)
  waiting for transfers between devices: 1020 us -> 60.6 us
  blocking collectives: 106 us -> 205 us
  starting transfers between devices: 15.1 us -> 105 us
  local copies, waits for them, and re-layouts: 122 us -> 70.3 us
  other arithmetic: 85.7 us -> 103 us
    reduce_scatter x8 -> x6, waiting for transfers between devices: 524 us -> 14.6 us  [reduced(): lax.psum_scatter(parts[0].astype(low), 'dp', scatter_dimension=0, tiled=T...]
    psum x5 -> x0, waiting for transfers between devices: 312 us -> none  [the longest x1 111 us: on_device(): lax.psum((sliced[0], sliced[1], sliced[2], sliced[3]), 'context')]
    all_gather x8 -> x0, waiting for transfers between devices: 184 us -> none  [the longest x2 111 us: on_device(): lax.all_gather(inner_proj[layer_index], 'dp', axis=0, tiled=True)]
    ppermute x8 -> x84, starting transfers between devices: 14.2 us -> 104 us  [the longest x68 80.3 us: swapped(): lax.ppermute(value, axis, [(i, i ^ bit) for i in range(lax.axis_size(axis...]
    psum x5 -> x2, blocking collectives: 31.2 us -> 101 us  [the longest x1 59.7 us: on_device(): lax.psum(tuple((v for i, v in enumerate(stacked) if i not in (3, 4))), ('...]
    ppermute x8 -> x84, waiting for transfers between devices: 2.92 us -> 45.9 us  [the longest x68 45 us: swapped(): lax.ppermute(value, axis, [(i, i ^ bit) for i in range(lax.axis_size(axis...]
    mul x28 -> x0, local copies, waits for them, and re-layouts: 36.5 us -> none  [the longest x12 9.13 us: link_states(): latter[0][:, :, None, None] * earlier[1] + latter[1]]
    all_gather x6, blocking collectives: 74.9 us -> 104 us  [on_device(): lax.all_gather(piece, 'dp', axis=0, tiled=True)]
  transfers between devices with their start and end apart: 29 -> 90, of which waited for: 21 -> 15; matrix products, arithmetic and copies ran while one was open for 12% -> 37% of each run, Pallas kernels for 0% -> 0%
where the time goes in v1:
time: 704 us; the launch traced here: 693 us
  blocking collectives  205 us (29%)
  matrix products  131 us (19%)
  starting transfers between devices  105 us (15%)
  other arithmetic  103 us (15%)
  local copies, waits for them, and re-layouts  70.3 us (10%)
  waiting for transfers between devices  60.6 us (9%)
  between operations  18.1 us (3%)
    all_gather x6, blocking collectives, on_device(): lax.all_gather(piece, 'dp', axis=0, tiled=True)  104 us
    ppermute x68, starting transfers between devices, swapped(): lax.ppermute(value, axis, [(i, i ^ bit) for i in range(lax.axis_size(axis...  80.3 us
    psum x1, blocking collectives, on_device(): lax.psum(tuple((v for i, v in enumerate(stacked) if i not in (3, 4))), ('...  59.7 us
    ppermute x68, waiting for transfers between devices, swapped(): lax.ppermute(value, axis, [(i, i ^ bit) for i in range(lax.axis_size(axis...  45 us
    psum x1, blocking collectives, on_device(): filters_grad, offsets_grad = lax.psum((stacked[3], stacked[4]), everywhere)  41.1 us
    dot_general x24, matrix products, product_grad(): lax.dot_general(part, values, (((0,), (0,)), ((), ())), preferred_element...  36.2 us
    dot_general x24, matrix products, product_out(): lax.dot_general(values, piece, (((1,), (1,)), ((), ())), preferred_elemen...  34.8 us
    dot_general x24, matrix products, product_in(): total = total + jnp.dot(part, piece, preferred_element_type=wide)  29.2 us
  transfers between devices with their start and end apart: 90, of which 15 were waited for; matrix products, arithmetic and copies ran while one was open for 37% of the time, Pallas kernels for 0%

profile of v1, /device:TPU:0, one launch (start us, length us, event | category | flops | bytes accessed | tf_op | source)
XLA Modules:
  0.0 692.6 jit_solution(12262494940512366329)
XLA Ops:
  8.6 18.0 %all_gather.23 = bf16[256,1024]{1,0:T(8,128)(2,1)} all-gather(bf16[64,1024]{1,0:T(8,128)(2,1)S(1)} %bitcast.586), channel_id=1, replica_groups=mesh['dp'=4,'context'=4,'tensor'=2] {'dp'}, dimensions={0}, use_global_device_ids=true | all-gather | bytes 655360 | tf_op jit(solution)/shard_map/all_gather | solution.py:339
  29.1 2.7 constant_dynamic-slice_fusion
  31.9 19.7 %all_gather.18 = bf16[256,1296]{1,0:T(8,128)(2,1)S(1)} all-gather(bf16[64,1296]{1,0:T(8,128)(2,1)S(1)} %pad_maximum_fusion.17), channel_id=1, replica_groups=mesh['dp'=4,'context'=4,'tensor'=2] {'dp'}, dimensions={0}, use_global_device_ids=true | all-gather | bytes 829440 | tf_op jit(solution)/shard_map/all_gather | solution.py:339
  53.3 16.5 %all-gather = bf16[1,256,1,1024]{3,1,2,0:T(8,128)(2,1)} all-gather(bf16[1,64,1,1024]{3,1,2,0:T(8,128)(2,1)S(1)} %copy.349), channel_id=2, replica_groups=mesh['dp'=4,'context'=4,'tensor'=2] {'dp'}, dimensions={1}, use_global_device_ids=true | all-gather | bytes 655360 | tf_op jit(solution)/shard_map/all_gather | solution.py:339
  77.0 16.4 %all_gather.20 = bf16[256,1024]{1,0:T(8,128)(2,1)} all-gather(bf16[64,1024]{1,0:T(8,128)(2,1)S(1)} %bitcast.587), channel_id=1, replica_groups=mesh['dp'=4,'context'=4,'tensor'=2] {'dp'}, dimensions={0}, use_global_device_ids=true | all-gather | bytes 655360 | tf_op jit(solution)/shard_map/all_gather | solution.py:339
  93.5 17.8 %all_gather.21 = bf16[256,1296]{1,0:T(8,128)(2,1)S(1)} all-gather(bf16[64,1296]{1,0:T(8,128)(2,1)S(1)} %pad_maximum_fusion.18), channel_id=1, replica_groups=mesh['dp'=4,'context'=4,'tensor'=2] {'dp'}, dimensions={0}, use_global_device_ids=true | all-gather | bytes 829440 | tf_op jit(solution)/shard_map/all_gather | solution.py:339
  128.4 3.4 fusion.55
  132.3 4.7 collective-permute-start.4
  142.8 10.5 %collective-permute-start.11 = (bf16[256,1024]{1,0:T(8,128)(2,1)S(1)}, bf16[256,1024]{1,0:T(8,128)(2,1)S(1)}, u32[]{:S(2)}, u32[]{:S(2)}) collective-permute-start(bf16[256,1024]{1,0:T(8,128)(2,1)S(1)} %copy-done.35), channel_id=1, source_target_pairs={{0,2},{2,0},{4,6},{6,4},{1,3},{3,1},{5,7},{7,5},{8,10},{10,8},{12,... | collective-permute-start | bytes 1572872 | tf_op jit(solution)/shard_map/ppermute | solution.py:12
  158.1 4.2 collective-permute-start.16
  167.6 16.1 %all-gather.1 = bf16[1,256,1,1024]{3,1,2,0:T(8,128)(2,1)} all-gather(bf16[1,64,1,1024]{3,1,2,0:T(8,128)(2,1)S(1)} %copy-done.138), channel_id=3, replica_groups=mesh['dp'=4,'context'=4,'tensor'=2] {'dp'}, dimensions={1}, use_global_device_ids=true | all-gather | bytes 655360 | tf_op jit(solution)/shard_map/all_gather | solution.py:339
  191.1 11.3 %collective-permute-done.23 = bf16[256,1024]{1,0:T(8,128)(2,1)} collective-permute-done((bf16[256,1024]{1,0:T(8,128)(2,1)}, bf16[256,1024]{1,0:T(8,128)(2,1)}, u32[]{:S(2)}, u32[]{:S(2)}) %collective-permute-start.23) | collective-permute-done | bytes 524320 | tf_op jit(solution)/shard_map/ppermute | solution.py:12
  212.5 5.9 fusion.54
  241.6 7.0 %collective-permute-done.25 = f32[256]{0:T(256)S(1)} collective-permute-done((f32[256]{0:T(256)S(1)}, f32[256]{0:T(256)S(1)}, u32[]{:S(2)}, u32[]{:S(2)}) %collective-permute-start.25) | collective-permute-done | bytes 1056 | tf_op jit(solution)/shard_map/ppermute | solution.py:12
  263.2 3.3 fusion.15
  273.8 2.8 collective-permute-start.52
  289.4 7.2 %collective-permute-start.54 = (bf16[256,1024]{1,0:T(8,128)(2,1)}, bf16[256,1024]{1,0:T(8,128)(2,1)}, u32[]{:S(2)}, u32[]{:S(2)}) collective-permute-start(bf16[256,1024]{1,0:T(8,128)(2,1)} %add_convert_fusion.9), channel_id=1, source_target_pairs={{0,4},{2,6},{4,0},{6,2},{1,5},{3,7},{5,1},{7,3},{8,12},{10,14},{12... | collective-permute-start | bytes 1572872 | tf_op jit(solution)/shard_map/ppermute | solution.py:12
  304.6 3.4 fusion.265
  347.9 6.7 collective-permute-done.34
  354.6 3.0 multiply_reduce_fusion.12
  357.7 2.7 multiply_reduce_fusion.16
  376.8 3.3 fusion.13
  405.5 2.8 collective-permute-start.60
  412.4 14.0 %collective-permute-start.42 = (bf16[256,1024]{1,0:T(8,128)(2,1)}, bf16[256,1024]{1,0:T(8,128)(2,1)}, u32[]{:S(2)}, u32[]{:S(2)}) collective-permute-start(bf16[256,1024]{1,0:T(8,128)(2,1)} %add_convert_fusion.11), channel_id=1, source_target_pairs={{0,4},{2,6},{4,0},{6,2},{1,5},{3,7},{5,1},{7,3},{8,12},{10,14},{12... | collective-permute-start | bytes 1572872 | tf_op jit(solution)/shard_map/ppermute | solution.py:12
  435.5 2.8 fusion.264
  443.0 2.9 pad_add_fusion
  461.9 41.1 %all-reduce.10 = (f32[2,4,256]{2,1,0:T(4,128)}, f32[2,256]{1,0:T(2,128)}) all-reduce(f32[2,4,256]{2,1,0:T(4,128)S(1)} %pad_maximum_fusion.29, f32[2,256]{1,0:T(2,128)S(1)} %pad_maximum_fusion.31), channel_id=1, replica_groups=mesh['dp'=4,'context'=4,'tensor'=2] {'dp','context','tensor'}, use_global_device_ids=true, to_apply=%region_51.52 | all-reduce | flops 2560 | bytes 20480 | tf_op jit(solution)/shard_map/psum | solution.py:368
  538.5 2.7 collective-permute-done.39
  559.8 8.5 %collective-permute-done.48 = bf16[256,1296]{0,1:T(8,128)(2,1)} collective-permute-done((bf16[256,1296]{0,1:T(8,128)(2,1)}, bf16[256,1296]{0,1:T(8,128)(2,1)}, u32[]{:S(2)}, u32[]{:S(2)}) %collective-permute-start.48) | collective-permute-done | bytes 663584 | tf_op jit(solution)/shard_map/ppermute | solution.py:12
  569.7 12.5 %reduce-scatter.13.cloned.1.call-done = bf16[64,1296]{1,0:T(8,128)(2,1)} async-done(((bf16[256,1296]{1,0:T(8,128)(2,1)}), bf16[64,1296]{1,0:T(8,128)(2,1)}) %reduce-scatter.13.cloned.1.call-update) | async-done | bytes 165904 | tf_op jit(solution)/shard_map/reduce_scatter | solution.py:45
  595.8 59.7 %all-reduce.11 = (f32[2,1024]{1,0:T(2,128)}, f32[2,4,1024]{2,1,0:T(4,128)}, f32[2,1024]{1,0:T(2,128)}, f32[2,16]{1,0:T(2,128)}, f32[2,16]{1,0:T(2,128)}, /*index=5*/f32[2,16]{1,0:T(2,128)}, f32[2,1024]{1,0:T(2,128)}) all-reduce(f32[2,1024]{1,0:T(2,128)S(1)} %pad_maximum_fusion.27, ...), channel_id=1, replica_groups=mesh['dp'=4,'context'=4,'tensor'=2] {'dp','context'}, use_global_device_ids=true, to_apply=%region_34.35 | all-reduce | flops 14432 | bytes 115456 | tf_op jit(solution)/shard_map/psum | solution.py:369
  679.4 5.2 copy.311
  (1032 shorter events, 335.6 us)
Async XLA Ops:
  7.2 503.7 %reduce-scatter.11.cloned.1.call-start = ((), (), s32[]{:S(2)}) async-start(), calls=%async_computation.8 | async-start | bytes 655360 | tf_op jit(solution)/shard_map/reduce_scatter | solution.py:45
  26.6 164.0 %collective-permute-start.27 = (bf16[256,1024]{1,0:T(8,128)(2,1)}, bf16[256,1024]{1,0:T(8,128)(2,1)}, u32[]{:S(2)}, u32[]{:S(2)}) collective-permute-start(bf16[256,1024]{1,0:T(8,128)(2,1)} %all_gather.23), channel_id=1, source_target_pairs={{0,4},{2,6},{4,0},{6,2},{1,5},{3,7},{5,1},{7,3},{8,12},{10,14},{12... | collective-permute-start | bytes 1572872 | tf_op jit(solution)/shard_map/ppermute | solution.py:12
  28.1 205.5 %collective-permute-start.26 = (bf16[256,1024]{1,0:T(8,128)(2,1)}, bf16[256,1024]{1,0:T(8,128)(2,1)}, u32[]{:S(2)}, u32[]{:S(2)}) collective-permute-start(bf16[256,1024]{1,0:T(8,128)(2,1)} %all_gather.23), channel_id=1, source_target_pairs={{0,2},{2,0},{4,6},{6,4},{1,3},{3,1},{5,7},{7,5},{8,10},{10,8},{12,... | collective-permute-start | bytes 1572872 | tf_op jit(solution)/shard_map/ppermute | solution.py:12
  52.7 61.8 %collective-permute-start.1 = (bf16[256,1296]{0,1:T(8,128)(2,1)}, bf16[256,1296]{0,1:T(8,128)(2,1)}, u32[]{:S(2)}, u32[]{:S(2)}) collective-permute-start(bf16[256,1296]{0,1:T(8,128)(2,1)} %copy.253), channel_id=1, source_target_pairs={{0,4},{2,6},{4,0},{6,2},{1,5},{3,7},{5,1},{7,3},{8,12},{10,14},{12... | collective-permute-start | bytes 1990664 | tf_op jit(solution)/shard_map/ppermute | solution.py:12
  53.2 63.8 %collective-permute-start = (bf16[256,1296]{0,1:T(8,128)(2,1)}, bf16[256,1296]{0,1:T(8,128)(2,1)}, u32[]{:S(2)}, u32[]{:S(2)}) collective-permute-start(bf16[256,1296]{0,1:T(8,128)(2,1)} %copy.253), channel_id=1, source_target_pairs={{0,2},{2,0},{4,6},{6,4},{1,3},{3,1},{5,7},{7,5},{8,10},{10,8},{12,... | collective-permute-start | bytes 1990664 | tf_op jit(solution)/shard_map/ppermute | solution.py:12
  69.8 70.9 %collective-permute-start.7 = (bf16[256,1024]{1,0:T(8,128)(2,1)}, bf16[256,1024]{1,0:T(8,128)(2,1)}, u32[]{:S(2)}, u32[]{:S(2)}) collective-permute-start(bf16[256,1024]{1,0:T(8,128)(2,1)} %bitcast.20), channel_id=1, source_target_pairs={{0,2},{2,0},{4,6},{6,4},{1,3},{3,1},{5,7},{7,5},{8,10},{10,8},{12,... | collective-permute-start | bytes 1572872 | tf_op jit(solution)/shard_map/ppermute | solution.py:12
  117.0 36.5 %collective-permute-start.8 = (bf16[256,1024]{1,0:T(8,128)(2,1)}, bf16[256,1024]{1,0:T(8,128)(2,1)}, u32[]{:S(2)}, u32[]{:S(2)}) collective-permute-start(bf16[256,1024]{1,0:T(8,128)(2,1)} %bitcast.20), channel_id=1, source_target_pairs={{0,4},{2,6},{4,0},{6,2},{1,5},{3,7},{5,1},{7,3},{8,12},{10,14},{12... | collective-permute-start | bytes 1572872 | tf_op jit(solution)/shard_map/ppermute | solution.py:12
  158.1 29.7 %collective-permute-start.16 = (bf16[256,1296]{0,1:T(8,128)(2,1)S(1)}, bf16[256,1296]{0,1:T(8,128)(2,1)S(1)}, u32[]{:S(2)}, u32[]{:S(2)}) collective-permute-start(bf16[256,1296]{0,1:T(8,128)(2,1)S(1)} %copy-done.134), channel_id=1, source_target_pairs={{0,4},{2,6},{4,0},{6,2},{1,5},{3,7},{5,1},{7,3},{8,12},{10,14},{12... | collective-permute-start | bytes 1990664 | tf_op jit(solution)/shard_map/ppermute | solution.py:12
  190.6 32.5 %collective-permute-start.22 = (bf16[256,1024]{1,0:T(8,128)(2,1)}, bf16[256,1024]{1,0:T(8,128)(2,1)}, u32[]{:S(2)}, u32[]{:S(2)}) collective-permute-start(bf16[256,1024]{1,0:T(8,128)(2,1)} %bitcast.39), channel_id=1, source_target_pairs={{0,2},{2,0},{4,6},{6,4},{1,3},{3,1},{5,7},{7,5},{8,10},{10,8},{12,... | collective-permute-start | bytes 1572872 | tf_op jit(solution)/shard_map/ppermute | solution.py:12
  202.5 32.6 %collective-permute-start.28 = (bf16[256,1024]{1,0:T(8,128)(2,1)}, bf16[256,1024]{1,0:T(8,128)(2,1)}, u32[]{:S(2)}, u32[]{:S(2)}) collective-permute-start(bf16[256,1024]{1,0:T(8,128)(2,1)} %collective-permute-done.27), channel_id=1, source_target_pairs={{0,2},{2,0},{4,6},{6,4},{1,3},{3,1},{5,7},{7,5},{8,10},{10,8},{12,... | collective-permute-start | bytes 1572872 | tf_op jit(solution)/shard_map/ppermute | solution.py:12
  273.8 60.1 %collective-permute-start.52 = (bf16[256,1024]{1,0:T(8,128)(2,1)}, bf16[256,1024]{1,0:T(8,128)(2,1)}, u32[]{:S(2)}, u32[]{:S(2)}) collective-permute-start(bf16[256,1024]{1,0:T(8,128)(2,1)} %convolution_convert_fusion.9), channel_id=1, source_target_pairs={{0,2},{2,0},{4,6},{6,4},{1,3},{3,1},{5,7},{7,5},{8,10},{10,8},{12,... | collective-permute-start | bytes 1572872 | tf_op jit(solution)/shard_map/ppermute | solution.py:12
  276.6 68.6 %collective-permute-start.78 = (bf16[256,1024]{1,0:T(8,128)(2,1)}, bf16[256,1024]{1,0:T(8,128)(2,1)}, u32[]{:S(2)}, u32[]{:S(2)}) collective-permute-start(bf16[256,1024]{1,0:T(8,128)(2,1)} %convolution_convert_fusion.5), channel_id=1, source_target_pairs={{0,2},{2,0},{4,6},{6,4},{1,3},{3,1},{5,7},{7,5},{8,10},{10,8},{12,... | collective-permute-start | bytes 1572872 | tf_op jit(solution)/shard_map/ppermute | solution.py:12
  289.4 44.5 %collective-permute-start.54 = (bf16[256,1024]{1,0:T(8,128)(2,1)}, bf16[256,1024]{1,0:T(8,128)(2,1)}, u32[]{:S(2)}, u32[]{:S(2)}) collective-permute-start(bf16[256,1024]{1,0:T(8,128)(2,1)} %add_convert_fusion.9), channel_id=1, source_target_pairs={{0,4},{2,6},{4,0},{6,2},{1,5},{3,7},{5,1},{7,3},{8,12},{10,14},{12... | collective-permute-start | bytes 1572872 | tf_op jit(solution)/shard_map/ppermute | solution.py:12
  299.3 45.9 %collective-permute-start.80 = (bf16[256,1024]{1,0:T(8,128)(2,1)}, bf16[256,1024]{1,0:T(8,128)(2,1)}, u32[]{:S(2)}, u32[]{:S(2)}) collective-permute-start(bf16[256,1024]{1,0:T(8,128)(2,1)} %add_convert_fusion.5), channel_id=1, source_target_pairs={{0,4},{2,6},{4,0},{6,2},{1,5},{3,7},{5,1},{7,3},{8,12},{10,14},{12... | collective-permute-start | bytes 1572872 | tf_op jit(solution)/shard_map/ppermute | solution.py:12
  336.3 181.0 %reduce-scatter.17.cloned.1.call-start = ((), (), s32[]{:S(2)}) async-start(), calls=%async_computation.11 | async-start | bytes 655360 | tf_op jit(solution)/shard_map/reduce_scatter | solution.py:45
  341.1 61.6 %collective-permute-start.59 = (bf16[256,1296]{0,1:T(8,128)(2,1)}, bf16[256,1296]{0,1:T(8,128)(2,1)}, u32[]{:S(2)}, u32[]{:S(2)}) collective-permute-start(bf16[256,1296]{0,1:T(8,128)(2,1)} %convolution_convert_fusion), channel_id=1, source_target_pairs={{0,2},{2,0},{4,6},{6,4},{1,3},{3,1},{5,7},{7,5},{8,10},{10,8},{12,... | collective-permute-start | bytes 1990664 | tf_op jit(solution)/shard_map/ppermute | solution.py:12
  343.7 56.4 %collective-permute-start.58 = (bf16[256,1296]{0,1:T(8,128)(2,1)}, bf16[256,1296]{0,1:T(8,128)(2,1)}, u32[]{:S(2)}, u32[]{:S(2)}) collective-permute-start(bf16[256,1296]{0,1:T(8,128)(2,1)} %convolution_convert_fusion.1), channel_id=1, source_target_pairs={{0,2},{2,0},{4,6},{6,4},{1,3},{3,1},{5,7},{7,5},{8,10},{10,8},{12,... | collective-permute-start | bytes 1990664 | tf_op jit(solution)/shard_map/ppermute | solution.py:12
  347.6 207.4 %reduce-scatter.7.cloned.1.call-start = ((), (), s32[]{:S(2)}) async-start(), calls=%async_computation.6 | async-start | bytes 655360 | tf_op jit(solution)/shard_map/reduce_scatter | solution.py:45
  385.1 125.7 %collective-permute-start.40 = (bf16[256,1024]{1,0:T(8,128)(2,1)}, bf16[256,1024]{1,0:T(8,128)(2,1)}, u32[]{:S(2)}, u32[]{:S(2)}) collective-permute-start(bf16[256,1024]{1,0:T(8,128)(2,1)} %convolution_convert_fusion.11), channel_id=1, source_target_pairs={{0,2},{2,0},{4,6},{6,4},{1,3},{3,1},{5,7},{7,5},{8,10},{10,8},{12,... | collective-permute-start | bytes 1572872 | tf_op jit(solution)/shard_map/ppermute | solution.py:12
  400.0 117.3 %collective-permute-start.72 = (bf16[256,1024]{1,0:T(8,128)(2,1)}, bf16[256,1024]{1,0:T(8,128)(2,1)}, u32[]{:S(2)}, u32[]{:S(2)}) collective-permute-start(bf16[256,1024]{1,0:T(8,128)(2,1)} %convolution_convert_fusion.7), channel_id=1, source_target_pairs={{0,2},{2,0},{4,6},{6,4},{1,3},{3,1},{5,7},{7,5},{8,10},{10,8},{12,... | collective-permute-start | bytes 1572872 | tf_op jit(solution)/shard_map/ppermute | solution.py:12
  405.5 121.2 %collective-permute-start.60 = (bf16[256,1296]{0,1:T(8,128)(2,1)}, bf16[256,1296]{0,1:T(8,128)(2,1)}, u32[]{:S(2)}, u32[]{:S(2)}) collective-permute-start(bf16[256,1296]{0,1:T(8,128)(2,1)} %add_convert_fusion.2), channel_id=1, source_target_pairs={{0,4},{2,6},{4,0},{6,2},{1,5},{3,7},{5,1},{7,3},{8,12},{10,14},{12... | collective-permute-start | bytes 1990664 | tf_op jit(solution)/shard_map/ppermute | solution.py:12
  412.4 98.6 %collective-permute-start.42 = (bf16[256,1024]{1,0:T(8,128)(2,1)}, bf16[256,1024]{1,0:T(8,128)(2,1)}, u32[]{:S(2)}, u32[]{:S(2)}) collective-permute-start(bf16[256,1024]{1,0:T(8,128)(2,1)} %add_convert_fusion.11), channel_id=1, source_target_pairs={{0,4},{2,6},{4,0},{6,2},{1,5},{3,7},{5,1},{7,3},{8,12},{10,14},{12... | collective-permute-start | bytes 1572872 | tf_op jit(solution)/shard_map/ppermute | solution.py:12
  453.6 49.4 %collective-permute-start.38 = (f32[3,1280]{1,0:T(4,128)S(1)}, f32[3,1280]{1,0:T(4,128)S(1)}, u32[]{:S(2)}, u32[]{:S(2)}) collective-permute-start(f32[3,1280]{1,0:T(4,128)S(1)} %copy.297), channel_id=1, source_target_pairs={{2,0},{4,2},{6,4},{3,1},{5,3},{7,5},{10,8},{12,10},{14,12},{11,9},... | collective-permute-start | bytes 46088 | tf_op jit(solution)/shard_map/ppermute | solution.py:17
  513.3 45.0 %reduce-scatter.15.cloned.1.call-start = ((), (), s32[]{:S(2)}) async-start(), calls=%async_computation.10 | async-start | bytes 655360 | tf_op jit(solution)/shard_map/reduce_scatter | solution.py:45
  521.9 60.3 %reduce-scatter.13.cloned.1.call-start = ((), (), s32[]{:S(2)}) async-start(), calls=%async_computation.9 | async-start | bytes 901120 | tf_op jit(solution)/shard_map/reduce_scatter | solution.py:45
  533.7 126.4 %reduce-scatter.9.cloned.1.call-start = ((), (), s32[]{:S(2)}) async-start(), calls=%async_computation.7 | async-start | bytes 901120 | tf_op jit(solution)/shard_map/reduce_scatter | solution.py:45
  555.0 38.3 %collective-permute-start.44 = (bf16[64,1024]{1,0:T(8,128)(2,1)}, bf16[64,1024]{1,0:T(8,128)(2,1)}, u32[]{:S(2)}, u32[]{:S(2)}) collective-permute-start(bf16[64,1024]{1,0:T(8,128)(2,1)} %reduce-scatter.7.cloned.1.call-done), channel_id=1, source_target_pairs={{0,4},{2,6},{4,0},{6,2},{1,5},{3,7},{5,1},{7,3},{8,12},{10,14},{12... | collective-permute-start | bytes 393224 | tf_op jit(solution)/shard_map/ppermute | solution.py:12
  558.4 97.2 %collective-permute-start.76 = (bf16[64,1024]{1,0:T(8,128)(2,1)}, bf16[64,1024]{1,0:T(8,128)(2,1)}, u32[]{:S(2)}, u32[]{:S(2)}) collective-permute-start(bf16[64,1024]{1,0:T(8,128)(2,1)} %reduce-scatter.15.cloned.1.call-done), channel_id=1, source_target_pairs={{0,4},{2,6},{4,0},{6,2},{1,5},{3,7},{5,1},{7,3},{8,12},{10,14},{12... | collective-permute-start | bytes 393224 | tf_op jit(solution)/shard_map/ppermute | solution.py:12
  589.6 66.5 %collective-permute-start.43 = (bf16[64,1024]{1,0:T(8,128)(2,1)}, bf16[64,1024]{1,0:T(8,128)(2,1)S(1)}, u32[]{:S(2)}, u32[]{:S(2)}) collective-permute-start(bf16[64,1024]{1,0:T(8,128)(2,1)} %reduce-scatter.7.cloned.1.call-done), channel_id=1, source_target_pairs={{0,2},{2,0},{4,6},{6,4},{1,3},{3,1},{5,7},{7,5},{8,10},{10,8},{12,... | collective-permute-start | bytes 393224 | tf_op jit(solution)/shard_map/ppermute | solution.py:12
  591.8 64.4 %collective-permute-start.62 = (bf16[64,1296]{1,0:T(8,128)(2,1)}, bf16[64,1296]{1,0:T(8,128)(2,1)}, u32[]{:S(2)}, u32[]{:S(2)}) collective-permute-start(bf16[64,1296]{1,0:T(8,128)(2,1)} %reduce-scatter.13.cloned.1.call-done), channel_id=1, source_target_pairs={{0,4},{2,6},{4,0},{6,2},{1,5},{3,7},{5,1},{7,3},{8,12},{10,14},{12... | collective-permute-start | bytes 497672 | tf_op jit(solution)/shard_map/ppermute | solution.py:12
  593.3 62.3 %collective-permute-start.71 = (bf16[64,256]{1,0:T(8,128)(2,1)S(1)}, bf16[64,256]{1,0:T(8,128)(2,1)S(1)}, u32[]{:S(2)}, u32[]{:S(2)}) collective-permute-start(bf16[64,256]{1,0:T(8,128)(2,1)S(1)} %collective-permute-done.70), channel_id=1, source_target_pairs={{0,2},{2,0},{4,6},{6,4},{1,3},{3,1},{5,7},{7,5},{8,10},{10,8},{12,... | collective-permute-start | bytes 98312 | tf_op jit(solution)/shard_map/ppermute | solution.py:12
  593.3 63.4 %collective-permute-start.45 = (bf16[64,1024]{1,0:T(8,128)(2,1)}, bf16[64,1024]{1,0:T(8,128)(2,1)S(1)}, u32[]{:S(2)}, u32[]{:S(2)}) collective-permute-start(bf16[64,1024]{1,0:T(8,128)(2,1)} %collective-permute-done.44), channel_id=1, source_target_pairs={{0,2},{2,0},{4,6},{6,4},{1,3},{3,1},{5,7},{7,5},{8,10},{10,8},{12,... | collective-permute-start | bytes 393224 | tf_op jit(solution)/shard_map/ppermute | solution.py:12
  (325 other events, 3285.1 us)
Sparse Core Ops, SparseCore 0:
  336.5 23.2 reduce-scatter.10
  362.0 20.0 reduce-scatter.16
  513.5 22.5 reduce-scatter.6
  538.2 20.1 reduce-scatter.14
  561.1 21.1 reduce-scatter.12
  585.8 20.9 reduce-scatter.8
